TPU v7x, 32 devices: a whole 2x2x4 slice. The times are simulated.
32 devices in a mesh: dof: 1, tm: 32 (over z, y, x, core).
Axes of the slice: x: 2, y: 2, z: 4, core: 2. Of those that a mesh axis runs over, the one named last changes fastest.
Arguments:
- snapshots: bfloat16 [8192, 2048], P('dof', 'tm')
- derivatives: bfloat16 [8192, 2048], P('dof', 'tm')
- basis: bfloat16 [8192, 512], P('dof'), may hold values from -0.0625 to 0.0625
Outputs:
- states: float32 [512, 2048], P('dof', 'tm')
- operator: float32 [512, 512], P('dof')
All inputs are finite; a program needn't handle non-finite values.
Results may differ from a plain program's by a relative error of at most 0.0003.
Values sent between devices are 32-bit elements; how exact they have to be, the bound alone decides.
A program may use at most 64 MiB of HBM per device.

v0:
```python
import jax
import jax.numpy as jnp
from jax import lax
from jax.sharding import PartitionSpec as P


def project(basis, field):
    return lax.dot_general(
        basis, field, (((0,), (0,)), ((), ())), preferred_element_type=jnp.float32
    )


def solve_rows(gram, cross_rows):
    factor = jnp.linalg.cholesky(gram)
    middle = lax.linalg.triangular_solve(factor, cross_rows.T, left_side=True, lower=True)
    solved = lax.linalg.triangular_solve(
        factor, middle, left_side=True, lower=True, transpose_a=True
    )
    return solved.T


def per_device(snapshots, derivatives, basis):
    count = snapshots.shape[1] * lax.axis_size("tm")
    width = basis.shape[1]
    rows = width // lax.axis_size("dof")
    start = lax.axis_index("dof") * rows
    local_states = project(basis, snapshots)
    local_rates = project(basis, derivatives)
    identity = 0.05 * jnp.eye(width, dtype=jnp.float32)
    states, rates = lax.psum((local_states, local_rates), "dof")
    gram_part = jnp.dot(states, states.T, precision=lax.Precision.HIGHEST)
    cross_part = jnp.dot(rates, states.T, precision=lax.Precision.HIGHEST)
    gram, cross = lax.psum((gram_part, cross_part), "tm")
    gram = gram / count + identity
    cross_rows = lax.dynamic_slice_in_dim(cross, start, rows, 0) / count
    state_out = lax.dynamic_slice_in_dim(states, start, rows, 0)
    return (state_out, solve_rows(gram, cross_rows))


def solution(mesh):
    placed = (P("dof", "tm"), P("dof", "tm"), P("dof", None))
    return jax.shard_map(
        per_device,
        mesh=mesh,
        in_specs=placed,
        out_specs=(P("dof", "tm"), P("dof", None)),
        check_vma=False,
    )
```

profile of v0, /device:TPU:0, one launch (start us, length us, event | category | flops | bytes accessed | tf_op | source)
XLA Modules:
  0.0 330.9 jit_solution(16239619807895934925)
XLA Ops:
  7.2 1.2 copy-done
  8.4 5.1 %fusion.51 = f32[512,64]{0,1:T(8,128)S(1)} fusion(bf16[8192,64]{0,1:T(8,128)(2,1)S(1)} %copy-done, bf16[8192,512]{1,0:T(8,128)(2,1)} %param.5), kind=kOutput, calls=%fused_computation.93 | convolution fusion | flops 536870912 | bytes 9568256 | tf_op jit(solution)/shard_map/dot_general | solution.py:8
  13.5 0.7 copy-done.1
  14.2 2.4 fusion.49
  16.6 2.0 fusion.48
  18.6 2.0 fusion.50
  20.7 136.8 %all-reduce.4.cloned.1.call-done = (f32[512,512]{0,1:T(8,128)}, f32[512,512]{0,1:T(8,128)}) async-done(((f32[512,512]{0,1:T(8,128)}, f32[512,512]{0,1:T(8,128)}), (f32[512,512]{0,1:T(8,128)}, f32[512,512]{0,1:T(8,128)})) %all-reduce.4.cloned.1.call-update) | async-done | bytes 2097168 | tf_op jit(solution)/shard_map/psum | solution.py:33
  157.5 2.8 multiply_bitcast_fusion
  160.7 1.5 fusion
  162.1 11.7 %cholesky.103 = f32[128,128]{1,0:T(8,128)S(1)} custom-call(f32[128,128]{1,0:T(8,128)S(1)} %cholesky.263), custom_call_target="Cholesky" | custom-call | tf_op jit(solution)/shard_map/jit(cholesky)/cholesky | solution.py:14
  173.9 0.7 copy.7
  174.6 9.8 %custom-call.32 = f32[1,128,128]{1,2,0:T(8,128)S(1)} custom-call(f32[1,128,128]{2,1,0:T(8,128)S(1)} %get-tuple-element.33), custom_call_target="InvertDiagBlocksLowerTriangular" | custom-call | tf_op jit(solution)/shard_map/jit(cholesky)/cholesky | solution.py:14
  185.5 11.7 %cholesky.215 = f32[128,128]{1,0:T(8,128)S(1)} custom-call(f32[128,128]{1,0:T(8,128)S(1)} %cholesky.267), custom_call_target="Cholesky" | custom-call | tf_op jit(solution)/shard_map/jit(cholesky)/cholesky | solution.py:14
  197.2 0.7 copy.9
  198.0 10.4 %custom-call.33 = f32[1,128,128]{1,2,0:T(8,128)} custom-call(f32[1,128,128]{2,1,0:T(8,128)S(1)} %get-tuple-element.31), custom_call_target="InvertDiagBlocksLowerTriangular" | custom-call | tf_op jit(solution)/shard_map/jit(cholesky)/cholesky | solution.py:14
  208.4 1.0 cholesky.222
  209.4 0.8 constant_dynamic-update-slice_fusion.2
  210.2 1.2 convolution_dynamic-update-slice_fusion
  212.0 11.7 %cholesky.236 = f32[128,128]{1,0:T(8,128)S(1)} custom-call(f32[128,128]{1,0:T(8,128)S(1)} %cholesky.272), custom_call_target="Cholesky" | custom-call | tf_op jit(solution)/shard_map/jit(cholesky)/cholesky | solution.py:14
  223.9 19.5 %custom-call.34 = f32[1,128,128]{1,2,0:T(8,128)S(1)} custom-call(f32[1,128,128]{2,1,0:T(8,128)S(1)} %get-tuple-element.29), custom_call_target="InvertDiagBlocksLowerTriangular" | custom-call | tf_op jit(solution)/shard_map/jit(cholesky)/cholesky | solution.py:14
  244.1 11.7 %cholesky.253 = f32[128,128]{1,0:T(8,128)S(1)} custom-call(f32[128,128]{1,0:T(8,128)S(1)} %convolution_subtract_fusion.8), custom_call_target="Cholesky" | custom-call | tf_op jit(solution)/shard_map/jit(cholesky)/cholesky | solution.py:14
  261.4 11.0 %while.1 = (s32[]{:T(128)}, f32[512,512]{0,1:T(8,128)S(1)}, s32[4,2]{0,1:T(2,128)S(1)}, f32[4,128,128]{2,1,0:T(8,128)}, s32[]{:T(128)}) while((s32[]{:T(128)}, f32[512,512]{0,1:T(8,128)S(1)}, s32[4,2]{0,1:T(2,128)S(1)}, f32[4,128,128]{2,1,0:T(8,128)}, s32[]{:T(128)}) %tuple.29), condition=%wide.while_cond, body=%wide.while_body.sunk | while | flops 2 | bytes 393329 | solution.py:16
  262.1 1.3 dynamic-slice.7
  264.8 1.3 dynamic-slice.7
  267.5 1.3 dynamic-slice.7
  270.3 1.3 dynamic-slice.7
  272.4 40.1 %custom-call.35 = f32[4,128,128]{1,2,0:T(8,128)S(1)} custom-call(f32[4,128,128]{2,1,0:T(8,128)} %get-tuple-element.9), custom_call_target="InvertDiagBlocksLowerTriangular" | custom-call | tf_op jit(solution)/shard_map/triangular_solve | solution.py:16
  312.5 1.4 fusion.17
  313.9 1.4 convolution_subtract_fusion.3
  315.7 1.4 convolution_subtract_fusion.2
  317.5 1.6 convolution_subtract_fusion.5
  322.6 1.3 copy.16
  (62 shorter events, 15.8 us)
Async XLA Ops:
  7.2 1.2 copy-start
  7.2 6.3 %copy-start.3 = (bf16[8192,64]{0,1:T(8,128)(2,1)S(1)}, bf16[8192,64]{0,1:T(8,128)(2,1)}, u32[]{:S(2)}) copy-start(bf16[8192,64]{0,1:T(8,128)(2,1)} %param.4) | copy-start | bytes 3145732
  7.2 150.3 %all-reduce.4.cloned.1.call-start = ((), (), s32[]{:S(2)}) async-start(), calls=%async_computation | async-start | bytes 4194304 | tf_op jit(solution)/shard_map/psum | solution.py:33
  8.4 5.8 %copy-start.1 = (bf16[8192,512]{1,0:T(8,128)(2,1)S(1)}, bf16[8192,512]{1,0:T(8,128)(2,1)}, u32[]{:S(2)}) copy-start(bf16[8192,512]{1,0:T(8,128)(2,1)} %param.5) | copy-start | bytes 25165828
  14.2 146.1 %copy-start.2 = (f32[512,64]{0,1:T(8,128)}, f32[512,64]{0,1:T(8,128)S(1)}, u32[]{:S(2)}) copy-start(f32[512,64]{0,1:T(8,128)S(1)} %fusion.51) | copy-start | bytes 393220
Sparse Core Ops, SparseCore 0:
  20.8 136.6 all-reduce.3
where the time goes:
time: 335 us; the launch traced here: 331 us
  waiting for transfers between devices  137 us (41%)
  other arithmetic  134 us (40%)
  matrix products  24.8 us (7%)
  local copies, waits for them, and re-layouts  18.1 us (5%)
  between operations  17.1 us (5%)
    psum x1, waiting for transfers between devices, per_device(): gram, cross = lax.psum((gram_part, cross_part), 'tm')  137 us
    another operation x15, other arithmetic, solve_rows(): factor = jnp.linalg.cholesky(gram)  89.4 us
    another operation x3, other arithmetic, solve_rows(): lax.linalg.triangular_solve(factor, middle, left_side=True, lower=True, t...  40.3 us
    another operation x20, local copies, waits for them, and re-layouts  10.9 us
    dot_general x2, matrix products, project(): lax.dot_general(basis, field, (((0,), (0,)), ((), ())), preferred_element...  7.47 us
    another operation x7, matrix products, solve_rows(): lax.linalg.triangular_solve(factor, cross_rows.T, left_side=True, lower=T...  7.03 us
  transfers between devices with their start and end apart: 1, of which 1 were waited for; matrix products, arithmetic and copies ran while one was open for 0% of the time, Pallas kernels for 0%

commit v1 on v0

--- a/solution.py
+++ b/solution.py
@@ -1,13 +1,235 @@
+import functools
+
 import jax
 import jax.numpy as jnp
 from jax import lax
+from jax.experimental import pallas as pl
+from jax.experimental.pallas import tpu as pltpu
 from jax.sharding import PartitionSpec as P
+
+B = 128
+PAN = 8
+MESH = pl.DeviceIdType.MESH
 
 
 def project(basis, field):
     return lax.dot_general(
         basis, field, (((0,), (0,)), ((), ())), preferred_element_type=jnp.float32
     )
+
+
+def split(x):
+    high = x.astype(jnp.bfloat16)
+    return high, (x - high.astype(jnp.float32)).astype(jnp.bfloat16)
+
+
+def dot3(a, b, dims):
+    mul = lambda x, y: lax.dot_general(
+        x, y, (dims, ((), ())), preferred_element_type=jnp.float32
+    )
+    return mul(a[0], b[0]) + (mul(a[0], b[1]) + mul(a[1], b[0]))
+
+
+NN = ((1,), (0,))
+NT = ((1,), (1,))
+
+
+def reduce_kernel(nb, states_ref, rates_ref, out_ref, acc, got1, got2, got3, send, recv):
+    r = nb * B
+    low = [(i, j) for i in range(nb) for j in range(i + 1)]
+    total = (len(low) + nb * nb) * B
+    half, quarter, piece = total // 2, total // 8, total // 32
+
+    me = lax.axis_index("tm")
+    core = me % 2
+    xy = (me // 2) % 4
+    z = me // 8
+
+    def dev(zz, qq, cc):
+        return (0, zz * 8 + qq * 2 + cc)
+
+    core_peer = dev(z, xy, 1 - core)
+    flips = [xy + 1 - 2 * (xy % 2), lax.rem(xy + 2, 4)]
+    flips.append(3 - xy)
+    xy_peers = [dev(z, q, core) for q in flips]
+    zs = [lax.rem(z + d, 4) for d in (1, 2, 3)]
+    z_peers = [dev(q, xy, core) for q in zs]
+
+    barrier = pltpu.get_barrier_semaphore()
+    for peer in [core_peer] + xy_peers + z_peers:
+        pl.semaphore_signal(barrier, inc=1, device_id=peer, device_id_type=MESH)
+    pl.semaphore_wait(barrier, 7)
+
+    s = split(states_ref[...])
+    d = split(rates_ref[...])
+    gram = dot3(s, s, NT)
+    cross = dot3(d, s, NT)
+    for n, (i, j) in enumerate(low):
+        acc[n * B : (n + 1) * B, :] = gram[i * B : (i + 1) * B, j * B : (j + 1) * B]
+    for j in range(nb):
+        base = len(low) * B + j * r
+        acc[base : base + r, :] = cross[:, j * B : (j + 1) * B]
+
+    def rows(ref, start, size):
+        return ref.at[pl.ds(pl.multiple_of(start, 8), size), :]
+
+    def copy(n, src, dst, peer):
+        c = pltpu.make_async_remote_copy(
+            src_ref=src, dst_ref=dst, send_sem=send.at[n], recv_sem=recv.at[n],
+            device_id=peer, device_id_type=MESH,
+        )
+        c.start()
+        return c
+
+    my_half = core * half
+    my_quarter = my_half + xy * quarter
+    my_piece = my_quarter + z * piece
+
+    first = copy(0, rows(acc, (1 - core) * half, half), got1, core_peer)
+    first.wait()
+    acc[pl.ds(pl.multiple_of(my_half, 8), half), :] += got1[...]
+
+    second = [
+        copy(1 + k, rows(acc, my_half + q * quarter, quarter), got2.at[k], xy_peers[k])
+        for k, q in enumerate(flips)
+    ]
+    for c in second:
+        c.wait()
+    acc[pl.ds(pl.multiple_of(my_quarter, 8), quarter), :] += got2[0] + got2[1] + got2[2]
+
+    third = [
+        copy(4 + k, rows(acc, my_quarter + q * piece, piece), got3.at[k], z_peers[k])
+        for k, q in enumerate(zs)
+    ]
+    for c in third:
+        c.wait()
+    out_ref[pl.ds(pl.multiple_of(my_piece, 8), piece), :] = (
+        acc[pl.ds(pl.multiple_of(my_piece, 8), piece), :] + got3[0] + got3[1] + got3[2]
+    )
+
+    part = rows(out_ref, my_piece, piece)
+    fourth = [copy(7 + k, part, part, z_peers[k]) for k in range(3)]
+    for c in fourth:
+        c.wait()
+    part5 = rows(out_ref, my_quarter, quarter)
+    fifth = [copy(10 + k, part5, part5, xy_peers[k]) for k in range(3)]
+    for c in fifth:
+        c.wait()
+    part6 = rows(out_ref, my_half, half)
+    copy(13, part6, part6, core_peer).wait()
+
+
+def reduce_sums(states, rates):
+    nb = states.shape[0] // B
+    total = (nb * (nb + 1) // 2 + nb * nb) * B
+    f32 = jnp.float32
+    vmem = pl.BlockSpec(memory_space=pltpu.VMEM)
+    return pl.pallas_call(
+        functools.partial(reduce_kernel, nb),
+        out_shape=jax.ShapeDtypeStruct((total, B), f32),
+        in_specs=[vmem] * 2,
+        out_specs=vmem,
+        scratch_shapes=[
+            pltpu.VMEM((total, B), f32),
+            pltpu.VMEM((total // 2, B), f32),
+            pltpu.VMEM((3, total // 8, B), f32),
+            pltpu.VMEM((3, total // 32, B), f32),
+            pltpu.SemaphoreType.DMA((14,)),
+            pltpu.SemaphoreType.DMA((14,)),
+        ],
+        compiler_params=pltpu.CompilerParams(
+            collective_id=0, has_side_effects=True, vmem_limit_bytes=32 * 2**20
+        ),
+    )(states, rates)
+
+
+def invert_block(block):
+    tiles = [block[t * PAN : (t + 1) * PAN, :] for t in range(B // PAN)]
+    lane = lax.broadcasted_iota(jnp.int32, (PAN, B), 1)
+    sub = lax.broadcasted_iota(jnp.int32, (PAN, B), 0)
+    wide = lambda x: jnp.broadcast_to(x, (PAN, B))
+    for p in range(B // PAN):
+        at = p * PAN
+        inside = (lane >= at) & (lane < at + PAN)
+        cols = [[wide(t[:, at + j : at + j + 1]) for j in range(PAN)] for t in tiles]
+        diag = cols[p]
+        u = jnp.where(inside, jnp.where(lane - at == sub, 1.0, 0.0), tiles[p])
+        for k in range(PAN):
+            hit = sub == k
+            inv = 1.0 / wide(diag[k][k : k + 1, :])
+            scale = jnp.where(hit, 0.0, diag[k])
+            row = wide(u[k : k + 1, :]) * inv
+            u = jnp.where(hit, row, u - scale * row)
+            for j in range(k + 1, PAN):
+                dj = wide(diag[j][k : k + 1, :]) * inv
+                diag[j] = jnp.where(hit, dj, diag[j] - scale * dj)
+        us = [wide(u[k : k + 1, :]) for k in range(PAN)]
+        for t in [(p + 1 + q) % (B // PAN) for q in range(B // PAN)]:
+            if t == p:
+                tiles[t] = u
+                continue
+            new = jnp.where(inside, 0.0, tiles[t])
+            for k in range(PAN):
+                new = new - cols[t][k] * us[k]
+            tiles[t] = new
+    return jnp.concatenate(tiles, axis=0)
+
+
+def solve_kernel(nb, count, sums_ref, out_ref):
+    r = nb * B
+    low = [(i, j) for i in range(nb) for j in range(i + 1)]
+    diag = jnp.where(
+        lax.broadcasted_iota(jnp.int32, (B, B), 0) == lax.broadcasted_iota(jnp.int32, (B, B), 1),
+        0.05, 0.0,
+    )
+    g = {}
+    for n, (i, j) in enumerate(low):
+        g[i, j] = sums_ref[n * B : (n + 1) * B, :] * (1.0 / count)
+        if i == j:
+            g[i, j] = g[i, j] + diag
+    c = []
+    for j in range(nb):
+        base = len(low) * B + j * r
+        c.append(sums_ref[base : base + r, :] * (1.0 / count))
+    low_factor, inverse = {}, []
+    for j in range(nb):
+        w = split(invert_block(g[j, j]))
+        inverse.append(w)
+        panel = {i: split(g[i, j]) for i in range(j + 1, nb)}
+        for i in range(j + 1, nb):
+            low_factor[i, j] = split(dot3(panel[i], w, NN))
+        for i in range(j + 1, nb):
+            for k in range(j + 1, i + 1):
+                g[i, k] = g[i, k] - dot3(low_factor[i, j], panel[k], NT)
+        c[j] = split(c[j])
+        for k in range(j + 1, nb):
+            c[k] = c[k] - dot3(c[j], low_factor[k, j], NT)
+    x = [None] * nb
+    for j in reversed(range(nb)):
+        x[j] = dot3(c[j], inverse[j], NN)
+        for i in range(j + 1, nb):
+            x[j] = x[j] - dot3(x[i], low_factor[i, j], NN)
+        out_ref[:, j * B : (j + 1) * B] = x[j]
+        x[j] = split(x[j])
+
+
+def solve_sums(sums, width, count):
+    vmem = pl.BlockSpec(memory_space=pltpu.VMEM)
+    return pl.pallas_call(
+        functools.partial(solve_kernel, width // B, count),
+        out_shape=jax.ShapeDtypeStruct((width, width), jnp.float32),
+        in_specs=[vmem],
+        out_specs=vmem,
+        compiler_params=pltpu.CompilerParams(vmem_limit_bytes=32 * 2**20),
+    )(sums)
+
+
+def fast(snapshots, derivatives, basis):
+    count = snapshots.shape[1] * lax.axis_size("tm")
+    states = project(basis, snapshots)
+    rates = project(basis, derivatives)
+    sums = reduce_sums(states, rates)
+    return states, solve_sums(sums, basis.shape[1], count)
 
 
 def solve_rows(gram, cross_rows):
@@ -19,7 +241,7 @@
     return solved.T
 
 
-def per_device(snapshots, derivatives, basis):
+def general(snapshots, derivatives, basis):
     count = snapshots.shape[1] * lax.axis_size("tm")
     width = basis.shape[1]
     rows = width // lax.axis_size("dof")
@@ -39,8 +261,9 @@
 
 def solution(mesh):
     placed = (P("dof", "tm"), P("dof", "tm"), P("dof", None))
+    one = mesh.shape["dof"] == 1 and mesh.shape["tm"] == 32
     return jax.shard_map(
-        per_device,
+        fast if one else general,
         mesh=mesh,
         in_specs=placed,
         out_specs=(P("dof", "tm"), P("dof", None)),

time: 335 us -> 83.8 us (0.25); the launches traced: 331 us -> 83.2 us
  waiting for transfers between devices: 137 us -> 0 us
  other arithmetic: 134 us -> 0 us
  Pallas kernels: 0 us -> 70.5 us
  local copies, waits for them, and re-layouts: 18.1 us -> 1.35 us
  between operations: 17.1 us -> 0.69 us
  matrix products: 24.8 us -> 10.7 us
    psum x1 -> x0, waiting for transfers between devices: 137 us -> none  [per_device(): gram, cross = lax.psum((gram_part, cross_part), 'tm')]
    another operation x18 -> x0, other arithmetic: 130 us -> none  [the longest x15 89.4 us: solve_rows(): factor = jnp.linalg.cholesky(gram)]
    pallas_call x0 -> x2, Pallas kernels: none -> 70.5 us  [the longest x1 42.6 us: reduce_sums(): pl.pallas_call(functools.partial(reduce_kernel, nb), out_shape=jax.ShapeD...]
    another operation x34 -> x0, local copies, waits for them, and re-layouts: 14.5 us -> none
    another operation x20 -> x0, matrix products: 13.3 us -> none  [the longest x7 7.03 us: solve_rows(): lax.linalg.triangular_solve(factor, cross_rows.T, left_side=True, lower=T...]
    dot_general x2 -> x0, matrix products: 4.01 us -> none  [the longest x1 2.01 us: per_device(): gram_part = jnp.dot(states, states.T, precision=lax.Precision.HIGHEST)]
  transfers between devices with their start and end apart: 1 -> 0, of which waited for: 1 -> 0; matrix products, arithmetic and copies ran while one was open for 0% -> 0% of each run, Pallas kernels for 0% -> 0%
where the time goes in v1:
time: 83.8 us; the launch traced here: 83.2 us
  Pallas kernels  70.5 us (84%)
  matrix products  10.7 us (13%)
  local copies, waits for them, and re-layouts  1.35 us (2%)
    pallas_call x1, Pallas kernels, reduce_sums(): pl.pallas_call(functools.partial(reduce_kernel, nb), out_shape=jax.ShapeD...  42.6 us
    pallas_call x1, Pallas kernels, solve_sums(): pl.pallas_call(functools.partial(solve_kernel, width // B, count), out_sh...  27.8 us
    dot_general x2, matrix products, project(): lax.dot_general(basis, field, (((0,), (0,)), ((), ())), preferred_element...  10.7 us

profile of v1, /device:TPU:0, one launch (start us, length us, event | category | flops | bytes accessed | tf_op | source)
XLA Modules:
  0.0 83.2 jit_solution(14633062070838052736)
XLA Ops:
  0.6 0.0 copy-start
  0.6 0.0 copy-start.2
  0.7 1.2 %copy-done = bf16[8192,64]{0,1:T(8,128)(2,1)S(1)} copy-done((bf16[8192,64]{0,1:T(8,128)(2,1)S(1)}, bf16[8192,64]{0,1:T(8,128)(2,1)}, u32[]{:S(2)}) %copy-start) | copy-done | bytes 1048600
  1.9 4.9 %fusion.1 = f32[512,64]{0,1:T(8,128)S(1)} fusion(bf16[8192,64]{0,1:T(8,128)(2,1)S(1)} %copy-done, bf16[8192,512]{1,0:T(8,128)(2,1)} %param.5), kind=kOutput, calls=%fused_computation.1 | convolution fusion | flops 536870912 | bytes 9568256 | tf_op jit(solution)/shard_map/dot_general | solution.py:16
  6.8 0.0 copy-start.1
  6.8 0.1 copy.5.states_ref
  6.9 0.0 copy-done.2
  7.0 5.7 %fusion.rates_ref = f32[512,64]{1,0:T(8,128)S(1)} fusion(bf16[8192,512]{1,0:T(8,128)(2,1)} %param.5, bf16[8192,64]{0,1:T(8,128)(2,1)S(1)} %copy-done.2), kind=kOutput, calls=%fused_computation | convolution fusion | flops 536870912 | bytes 9568256 | tf_op jit(solution)/shard_map/dot_general | solution.py:16
  12.7 42.6 %shard_map.50.sums_ref = f32[3328,128]{1,0:T(8,128)S(1)} custom-call(f32[512,64]{1,0:T(8,128)S(1)} %copy.5.states_ref, f32[512,64]{1,0:T(8,128)S(1)} %fusion.rates_ref), custom_call_target="tpu_custom_call" | custom-call | tf_op jit(solution)/shard_map/pallas_call | solution.py:127
  55.3 27.8 %shard_map.51 = f32[512,512]{1,0:T(8,128)} custom-call(f32[3328,128]{1,0:T(8,128)S(1)} %shard_map.50.sums_ref), custom_call_target="tpu_custom_call" | custom-call | tf_op jit(solution)/shard_map/pallas_call | solution.py:218
  83.2 0.0 copy-done.1
Async XLA Ops:
  0.6 1.2 %copy-start = (bf16[8192,64]{0,1:T(8,128)(2,1)S(1)}, bf16[8192,64]{0,1:T(8,128)(2,1)}, u32[]{:S(2)}) copy-start(bf16[8192,64]{0,1:T(8,128)(2,1)} %param.3) | copy-start | bytes 3145732
  0.6 6.3 %copy-start.2 = (bf16[8192,64]{0,1:T(8,128)(2,1)S(1)}, bf16[8192,64]{0,1:T(8,128)(2,1)}, u32[]{:S(2)}) copy-start(bf16[8192,64]{0,1:T(8,128)(2,1)} %param.4) | copy-start | bytes 3145732
  6.8 76.4 %copy-start.1 = (f32[512,64]{0,1:T(8,128)}, f32[512,64]{0,1:T(8,128)S(1)}, u32[]{:S(2)}) copy-start(f32[512,64]{0,1:T(8,128)S(1)} %fusion.1) | copy-start | bytes 393220

commit v2 on v0

--- a/solution.py
+++ b/solution.py
@@ -1,13 +1,313 @@
+import functools
+
 import jax
 import jax.numpy as jnp
 from jax import lax
+from jax.experimental import pallas as pl
+from jax.experimental.pallas import tpu as pltpu
 from jax.sharding import PartitionSpec as P
+
+B = 128
+PAN = 8
+MESH = pl.DeviceIdType.MESH
 
 
 def project(basis, field):
     return lax.dot_general(
         basis, field, (((0,), (0,)), ((), ())), preferred_element_type=jnp.float32
     )
+
+
+def split(x):
+    high = x.astype(jnp.bfloat16)
+    return high, (x - high.astype(jnp.float32)).astype(jnp.bfloat16)
+
+
+def dot3(a, b, dims):
+    mul = lambda x, y: lax.dot_general(
+        x, y, (dims, ((), ())), preferred_element_type=jnp.float32
+    )
+    return mul(a[0], b[0]) + (mul(a[0], b[1]) + mul(a[1], b[0]))
+
+
+NN = ((1,), (0,))
+NT = ((1,), (1,))
+TN = ((0,), (0,))
+
+
+def project_kernel(fields_a, fields_b, basis, states_ref, rates_ref):
+    @pl.when(pl.program_id(0) == 0)
+    def _():
+        states_ref[...] = jnp.zeros_like(states_ref)
+        rates_ref[...] = jnp.zeros_like(rates_ref)
+
+    n = fields_a.shape[0]
+    both = jnp.concatenate([fields_a[...], fields_b[...]], axis=0)
+    part = jnp.dot(both, basis[...], preferred_element_type=jnp.float32)
+    states_ref[...] += part[:n]
+    rates_ref[...] += part[n:]
+
+
+def project_both(snapshots_t, derivatives_t, basis, chunk=1024):
+    n, depth = snapshots_t.shape
+    width = basis.shape[1]
+    field = pl.BlockSpec((n, chunk), lambda i: (0, i))
+    result = pl.BlockSpec((n, width), lambda i: (0, 0))
+    return pl.pallas_call(
+        project_kernel,
+        grid=(depth // chunk,),
+        out_shape=[jax.ShapeDtypeStruct((n, width), jnp.float32)] * 2,
+        in_specs=[field, field, pl.BlockSpec((chunk, width), lambda i: (i, 0))],
+        out_specs=[result, result],
+        compiler_params=pltpu.CompilerParams(vmem_limit_bytes=56 * 2**20),
+    )(snapshots_t, derivatives_t, basis)
+
+
+def lower_blocks(nb):
+    return [(i, j) for i in range(nb) for j in range(i + 1)]
+
+
+def aligned(ref, start, size):
+    return ref.at[pl.ds(pl.multiple_of(start, 8), size), :]
+
+
+class AllReduce:
+    def __init__(self, place, acc, out, got, send, recv):
+        self.core, self.xy, self.z, self.peers = place
+        self.acc, self.out, self.got, self.send, self.recv = acc, out, got, send, recv
+        total = acc.shape[0]
+        self.half, self.quarter, self.piece = total // 2, total // 8, total // 32
+        self.my_half = self.core * self.half
+        self.my_quarter = self.my_half + self.xy * self.quarter
+        self.my_piece = self.my_quarter + self.z * self.piece
+        self.flying = []
+
+    def start(self, first, pairs, peers):
+        for k, (src, dst) in enumerate(pairs):
+            n = first + k
+            c = pltpu.make_async_remote_copy(
+                src_ref=src, dst_ref=dst, send_sem=self.send.at[n],
+                recv_sem=self.recv.at[n], device_id=peers[k], device_id_type=MESH,
+            )
+            c.start()
+            self.flying.append(c)
+
+    def land(self):
+        for c in self.flying:
+            c.wait()
+        self.flying = []
+
+    def step(self, n):
+        self.land()
+        acc, out, got = self.acc, self.out, self.got
+        core_peer, (flips, xy_peers), (zs, z_peers) = self.peers
+        if n == 0:
+            src = aligned(acc, (1 - self.core) * self.half, self.half)
+            self.start(0, [(src, got[0])], [core_peer])
+        elif n == 1:
+            aligned(acc, self.my_half, self.half)[...] += got[0][...]
+            self.start(1, [
+                (aligned(acc, self.my_half + q * self.quarter, self.quarter), got[1].at[k])
+                for k, q in enumerate(flips)
+            ], xy_peers)
+        elif n == 2:
+            aligned(acc, self.my_quarter, self.quarter)[...] += (
+                got[1][0] + got[1][1] + got[1][2]
+            )
+            self.start(4, [
+                (aligned(acc, self.my_quarter + q * self.piece, self.piece), got[2].at[k])
+                for k, q in enumerate(zs)
+            ], z_peers)
+        elif n == 3:
+            part = aligned(out, self.my_piece, self.piece)
+            part[...] = (
+                aligned(acc, self.my_piece, self.piece)[...]
+                + got[2][0] + got[2][1] + got[2][2]
+            )
+            self.start(7, [(part, part)] * 3, z_peers)
+        elif n == 4:
+            part = aligned(out, self.my_quarter, self.quarter)
+            self.start(10, [(part, part)] * 3, xy_peers)
+        elif n == 5:
+            part = aligned(out, self.my_half, self.half)
+            self.start(13, [(part, part)], [core_peer])
+
+
+def invert_block(block, hook):
+    np_ = B // PAN
+    tiles = block.reshape(np_, PAN, B)
+    lane = lax.broadcasted_iota(jnp.int32, (PAN, B), 1)
+    sub = lax.broadcasted_iota(jnp.int32, (PAN, B), 0)
+    wide = lambda x: jnp.broadcast_to(x, (PAN, B))
+    for p in range(np_):
+        hook(p)
+        at = p * PAN
+        inside = (lane >= at) & (lane < at + PAN)
+        cols = [
+            jnp.broadcast_to(tiles[:, :, at + j : at + j + 1], (np_, PAN, B))
+            for j in range(PAN)
+        ]
+        diag = jnp.stack([c[p] for c in cols])
+        u = jnp.where(inside, jnp.where(lane - at == sub, 1.0, 0.0), tiles[p])
+        for k in range(PAN):
+            hit = sub == k
+            pivot = diag[0]
+            inv = 1.0 / wide(pivot[k : k + 1, :])
+            scale = jnp.where(hit, 0.0, pivot)
+            row = wide(u[k : k + 1, :]) * inv
+            u = jnp.where(hit, row, u - scale * row)
+            if k < PAN - 1:
+                diag = diag[1:]
+                head = jnp.broadcast_to(diag[:, k : k + 1, :], diag.shape) * inv[None]
+                diag = jnp.where(hit[None], head, diag - scale[None] * head)
+        new = jnp.where(inside[None], 0.0, tiles)
+        for k in range(PAN):
+            new = new - cols[k] * wide(u[k : k + 1, :])[None]
+        parts = [new[:p]] if p else []
+        parts += [u[None]] + ([new[p + 1 :]] if p + 1 < np_ else [])
+        tiles = jnp.concatenate(parts, axis=0)
+    return tiles.reshape(B, B)
+
+
+def factor_blocks(nb, count, sums_ref, out_ref, hook):
+    diag = jnp.where(
+        lax.broadcasted_iota(jnp.int32, (B, B), 0) == lax.broadcasted_iota(jnp.int32, (B, B), 1),
+        0.05, 0.0,
+    )
+    index = {ij: n * B for n, ij in enumerate(lower_blocks(nb))}
+    g = {}
+    for (i, j), n in index.items():
+        g[i, j] = sums_ref[n : n + B, :] * (1.0 / count)
+        if i == j:
+            g[i, j] = g[i, j] + diag
+    for j in range(nb):
+        w = invert_block(g[j, j], functools.partial(hook, j))
+        out_ref[index[j, j] : index[j, j] + B, :] = w
+        w = split(w)
+        panel = {i: split(g[i, j]) for i in range(j + 1, nb)}
+        for i in range(j + 1, nb):
+            low = dot3(panel[i], w, NN)
+            out_ref[index[i, j] : index[i, j] + B, :] = low
+            low = split(low)
+            for k in range(j + 1, i + 1):
+                g[i, k] = g[i, k] - dot3(low, panel[k], NT)
+
+
+def sums_kernel(
+    nb, count, states_ref, rates_ref, factor_ref, cross_ref,
+    acc_g, out_g, g0, g1, g2, acc_c, c0, c1, c2, send_g, recv_g, send_c, recv_c,
+):
+    r = nb * B
+    me = lax.axis_index("tm")
+    core, xy, z = me % 2, (me // 2) % 4, me // 8
+
+    def dev(zz, qq, cc):
+        return (0, zz * 8 + qq * 2 + cc)
+
+    flips = [xy + 1 - 2 * (xy % 2), (xy + 2) % 4, 3 - xy]
+    zs = [(z + d) % 4 for d in (1, 2, 3)]
+    core_peer = dev(z, xy, 1 - core)
+    xy_peers = [dev(z, q, core) for q in flips]
+    z_peers = [dev(q, xy, core) for q in zs]
+    place = (core, xy, z, (core_peer, (flips, xy_peers), (zs, z_peers)))
+
+    barrier = pltpu.get_barrier_semaphore()
+    for peer in [core_peer] + xy_peers + z_peers:
+        pl.semaphore_signal(barrier, inc=1, device_id=peer, device_id_type=MESH)
+
+    s = split(states_ref[...])
+    gram = dot3(s, s, TN)
+    for n, (i, j) in enumerate(lower_blocks(nb)):
+        acc_g[n * B : (n + 1) * B, :] = gram[i * B : (i + 1) * B, j * B : (j + 1) * B]
+    pl.semaphore_wait(barrier, 7)
+
+    of_gram = AllReduce(place, acc_g, out_g, (g0, g1, g2), send_g, recv_g)
+    of_cross = AllReduce(place, acc_c, cross_ref, (c0, c1, c2), send_c, recv_c)
+    of_gram.step(0)
+    d = split(rates_ref[...])
+    cross = dot3(d, s, TN)
+    for j in range(nb):
+        acc_c[j * r : (j + 1) * r, :] = cross[:, j * B : (j + 1) * B]
+    of_gram.step(1)
+    of_cross.step(0)
+    for n in range(2, 6):
+        of_gram.step(n)
+    of_cross.step(1)
+    of_gram.land()
+
+    steps = {(1, 0): 2, (1, B // PAN // 2): 3, (2, 0): 4, (3, 0): 5}
+
+    def hook(j, p):
+        if (j, p) in steps:
+            of_cross.step(steps[j, p])
+
+    factor_blocks(nb, count, out_g, factor_ref, hook)
+    of_cross.land()
+
+
+def sums_and_factor(states_t, rates_t, count):
+    width = states_t.shape[1]
+    nb = width // B
+    f32 = jnp.float32
+    gram, cross = nb * (nb + 1) // 2 * B, nb * nb * B
+    vmem = pl.BlockSpec(memory_space=pltpu.VMEM)
+
+    def landing(total):
+        return [
+            pltpu.VMEM((total // 2, B), f32),
+            pltpu.VMEM((3, total // 8, B), f32),
+            pltpu.VMEM((3, total // 32, B), f32),
+        ]
+
+    return pl.pallas_call(
+        functools.partial(sums_kernel, nb, count),
+        out_shape=[jax.ShapeDtypeStruct((gram, B), f32), jax.ShapeDtypeStruct((cross, B), f32)],
+        in_specs=[vmem] * 2,
+        out_specs=[vmem] * 2,
+        scratch_shapes=[pltpu.VMEM((gram, B), f32)] * 2
+        + landing(gram)
+        + [pltpu.VMEM((cross, B), f32)]
+        + landing(cross)
+        + [pltpu.SemaphoreType.DMA((14,))] * 4,
+        compiler_params=pltpu.CompilerParams(
+            collective_id=0, has_side_effects=True, vmem_limit_bytes=32 * 2**20
+        ),
+    )(states_t, rates_t)
+
+
+def substitute_kernel(nb, count, factor_ref, cross_ref, out_ref):
+    r = nb * B
+    index = {ij: n * B for n, ij in enumerate(lower_blocks(nb))}
+    f = {ij: split(factor_ref[n : n + B, :]) for ij, n in index.items()}
+    c = [cross_ref[j * r : (j + 1) * r, :] * (1.0 / count) for j in range(nb)]
+    for j in range(nb):
+        c[j] = split(c[j])
+        for k in range(j + 1, nb):
+            c[k] = c[k] - dot3(c[j], f[k, j], NT)
+    x = [dot3(c[j], f[j, j], NN) for j in range(nb)]
+    for j in reversed(range(nb)):
+        out_ref[:, j * B : (j + 1) * B] = x[j]
+        done = split(x[j])
+        for k in range(j):
+            x[k] = x[k] - dot3(done, f[j, k], NN)
+
+
+def substitute(factor, cross, width, count):
+    vmem = pl.BlockSpec(memory_space=pltpu.VMEM)
+    return pl.pallas_call(
+        functools.partial(substitute_kernel, width // B, count),
+        out_shape=jax.ShapeDtypeStruct((width, width), jnp.float32),
+        in_specs=[vmem] * 2,
+        out_specs=vmem,
+        compiler_params=pltpu.CompilerParams(vmem_limit_bytes=32 * 2**20),
+    )(factor, cross)
+
+
+def fast(snapshots, derivatives, basis):
+    count = snapshots.shape[1] * lax.axis_size("tm")
+    states_t, rates_t = project_both(snapshots.T, derivatives.T, basis)
+    factor, cross = sums_and_factor(states_t, rates_t, count)
+    return states_t.T, substitute(factor, cross, basis.shape[1], count)
 
 
 def solve_rows(gram, cross_rows):
@@ -19,7 +319,7 @@
     return solved.T
 
 
-def per_device(snapshots, derivatives, basis):
+def general(snapshots, derivatives, basis):
     count = snapshots.shape[1] * lax.axis_size("tm")
     width = basis.shape[1]
     rows = width // lax.axis_size("dof")
@@ -39,8 +339,9 @@
 
 def solution(mesh):
     placed = (P("dof", "tm"), P("dof", "tm"), P("dof", None))
+    one = mesh.shape["dof"] == 1 and mesh.shape["tm"] == 32
     return jax.shard_map(
-        per_device,
+        fast if one else general,
         mesh=mesh,
         in_specs=placed,
         out_specs=(P("dof", "tm"), P("dof", None)),

time: 335 us -> 79.4 us (0.24); the launches traced: 331 us -> 79.1 us
  waiting for transfers between devices: 137 us -> 0 us
  other arithmetic: 134 us -> 0 us
  Pallas kernels: 0 us -> 76.7 us
  matrix products: 24.8 us -> 0 us
  between operations: 17.1 us -> 0.64 us
  local copies, waits for them, and re-layouts: 18.1 us -> 1.81 us
    psum x1 -> x0, waiting for transfers between devices: 137 us -> none  [per_device(): gram, cross = lax.psum((gram_part, cross_part), 'tm')]
    another operation x18 -> x0, other arithmetic: 130 us -> none  [the longest x15 89.4 us: solve_rows(): factor = jnp.linalg.cholesky(gram)]
    pallas_call x0 -> x3, Pallas kernels: none -> 76.7 us  [the longest x1 65.4 us: sums_and_factor(): pl.pallas_call(functools.partial(sums_kernel, nb, count), out_shape=[jax....]
    another operation x34 -> x0, local copies, waits for them, and re-layouts: 14.5 us -> none
    another operation x20 -> x0, matrix products: 13.3 us -> none  [the longest x7 7.03 us: solve_rows(): lax.linalg.triangular_solve(factor, cross_rows.T, left_side=True, lower=T...]
    dot_general x4 -> x0, matrix products: 11.5 us -> none  [the longest x2 7.47 us: project(): lax.dot_general(basis, field, (((0,), (0,)), ((), ())), preferred_element...]
  transfers between devices with their start and end apart: 1 -> 0, of which waited for: 1 -> 0; matrix products, arithmetic and copies ran while one was open for 0% -> 0% of each run, Pallas kernels for 0% -> 0%
where the time goes in v2:
time: 79.4 us; the launch traced here: 79.1 us
  Pallas kernels  76.7 us (97%)
  local copies, waits for them, and re-layouts  1.81 us (2%)
    pallas_call x1, Pallas kernels, sums_and_factor(): pl.pallas_call(functools.partial(sums_kernel, nb, count), out_shape=[jax....  65.4 us
    pallas_call x1, Pallas kernels, project_both(): pl.pallas_call(project_kernel, grid=(depth // chunk,), out_shape=[jax.Sha...  7.96 us
    pallas_call x1, Pallas kernels, substitute(): pl.pallas_call(functools.partial(substitute_kernel, width // B, count), o...  3.34 us
    unnamed x4, local copies, waits for them, and re-layouts  1.81 us

profile of v2, /device:TPU:0, one launch (start us, length us, event | category | flops | bytes accessed | tf_op | source)
XLA Modules:
  0.0 79.1 jit_solution(8841636488324939574)
XLA Ops:
  0.6 8.0 %shard_map.50 = (f32[64,512]{1,0:T(8,128)}, f32[64,512]{1,0:T(8,128)}) custom-call(bf16[64,8192]{1,0:T(8,128)(2,1)} %bitcast.4, bf16[64,8192]{1,0:T(8,128)(2,1)} %bitcast.5, bf16[8192,512]{1,0:T(8,128)(2,1)} %basis.1), custom_call_target="tpu_custom_call" | custom-call | tf_op jit(solution)/shard_map/pallas_call | solution.py:56
  8.6 0.0 copy-start
  8.6 0.9 %copy-done = f32[64,512]{1,0:T(8,128)S(1)} copy-done((f32[64,512]{1,0:T(8,128)S(1)}, f32[64,512]{1,0:T(8,128)}, u32[]{:S(2)}) %copy-start) | copy-done | bytes 131096
  9.5 0.0 copy-start.1
  9.5 0.9 %copy-done.1 = f32[64,512]{1,0:T(8,128)S(1)} copy-done((f32[64,512]{1,0:T(8,128)S(1)}, f32[64,512]{1,0:T(8,128)}, u32[]{:S(2)}) %copy-start.1) | copy-done | bytes 131096
  10.4 65.4 %shard_map.51 = (f32[1280,128]{1,0:T(8,128)S(1)}, f32[2048,128]{1,0:T(8,128)S(1)}) custom-call(f32[64,512]{1,0:T(8,128)S(1)} %copy-done, f32[64,512]{1,0:T(8,128)S(1)} %copy-done.1), custom_call_target="tpu_custom_call" | custom-call | tf_op jit(solution)/shard_map/pallas_call | solution.py:262
  75.8 3.3 %shard_map.52 = f32[512,512]{1,0:T(8,128)} custom-call(f32[1280,128]{1,0:T(8,128)S(1)} %get-tuple-element.8.factor_ref, f32[2048,128]{1,0:T(8,128)S(1)} %get-tuple-element.9.cross_ref), custom_call_target="tpu_custom_call" | custom-call | tf_op jit(solution)/shard_map/pallas_call | solution.py:297
Async XLA Ops:
  8.6 0.9 %copy-start = (f32[64,512]{1,0:T(8,128)S(1)}, f32[64,512]{1,0:T(8,128)}, u32[]{:S(2)}) copy-start(f32[64,512]{1,0:T(8,128)} %get-tuple-element.6.states_ref) | copy-start | bytes 393220
  9.5 0.9 %copy-start.1 = (f32[64,512]{1,0:T(8,128)S(1)}, f32[64,512]{1,0:T(8,128)}, u32[]{:S(2)}) copy-start(f32[64,512]{1,0:T(8,128)} %get-tuple-element.7.rates_ref) | copy-start | bytes 393220

commit v3 on v2

--- a/solution.py
+++ b/solution.py
@@ -35,30 +35,30 @@
 TN = ((0,), (0,))
 
 
-def project_kernel(fields_a, fields_b, basis, states_ref, rates_ref):
+def project_kernel(fields_a, fields_b, basis, states_ref, both_ref):
     @pl.when(pl.program_id(0) == 0)
     def _():
-        states_ref[...] = jnp.zeros_like(states_ref)
-        rates_ref[...] = jnp.zeros_like(rates_ref)
-
-    n = fields_a.shape[0]
+        both_ref[...] = jnp.zeros_like(both_ref)
+
     both = jnp.concatenate([fields_a[...], fields_b[...]], axis=0)
-    part = jnp.dot(both, basis[...], preferred_element_type=jnp.float32)
-    states_ref[...] += part[:n]
-    rates_ref[...] += part[n:]
-
-
-def project_both(snapshots_t, derivatives_t, basis, chunk=1024):
+    both_ref[...] += jnp.dot(both, basis[...], preferred_element_type=jnp.float32)
+
+    @pl.when(pl.program_id(0) == pl.num_programs(0) - 1)
+    def _():
+        states_ref[...] = both_ref[: states_ref.shape[0], :]
+
+
+def project_both(snapshots_t, derivatives_t, basis, chunk=2048):
     n, depth = snapshots_t.shape
     width = basis.shape[1]
     field = pl.BlockSpec((n, chunk), lambda i: (0, i))
-    result = pl.BlockSpec((n, width), lambda i: (0, 0))
+    result = lambda rows: pl.BlockSpec((rows, width), lambda i: (0, 0))
     return pl.pallas_call(
         project_kernel,
         grid=(depth // chunk,),
-        out_shape=[jax.ShapeDtypeStruct((n, width), jnp.float32)] * 2,
+        out_shape=[jax.ShapeDtypeStruct((k * n, width), jnp.float32) for k in (1, 2)],
         in_specs=[field, field, pl.BlockSpec((chunk, width), lambda i: (i, 0))],
-        out_specs=[result, result],
+        out_specs=[result(n), result(2 * n)],
         compiler_params=pltpu.CompilerParams(vmem_limit_bytes=56 * 2**20),
     )(snapshots_t, derivatives_t, basis)
 
@@ -194,7 +194,7 @@
 
 
 def sums_kernel(
-    nb, count, states_ref, rates_ref, factor_ref, cross_ref,
+    nb, count, both_ref, factor_ref, cross_ref,
     acc_g, out_g, g0, g1, g2, acc_c, c0, c1, c2, send_g, recv_g, send_c, recv_c,
 ):
     r = nb * B
@@ -215,7 +215,8 @@
     for peer in [core_peer] + xy_peers + z_peers:
         pl.semaphore_signal(barrier, inc=1, device_id=peer, device_id_type=MESH)
 
-    s = split(states_ref[...])
+    n_local = both_ref.shape[0] // 2
+    s = split(both_ref[:n_local, :])
     gram = dot3(s, s, TN)
     for n, (i, j) in enumerate(lower_blocks(nb)):
         acc_g[n * B : (n + 1) * B, :] = gram[i * B : (i + 1) * B, j * B : (j + 1) * B]
@@ -224,18 +225,21 @@
     of_gram = AllReduce(place, acc_g, out_g, (g0, g1, g2), send_g, recv_g)
     of_cross = AllReduce(place, acc_c, cross_ref, (c0, c1, c2), send_c, recv_c)
     of_gram.step(0)
-    d = split(rates_ref[...])
+    of_gram.step(1)
+    d = split(both_ref[n_local:, :])
     cross = dot3(d, s, TN)
     for j in range(nb):
         acc_c[j * r : (j + 1) * r, :] = cross[:, j * B : (j + 1) * B]
-    of_gram.step(1)
     of_cross.step(0)
-    for n in range(2, 6):
-        of_gram.step(n)
+    of_gram.step(2)
+    of_gram.step(3)
     of_cross.step(1)
+    of_gram.step(4)
+    of_gram.step(5)
+    of_cross.step(2)
     of_gram.land()
 
-    steps = {(1, 0): 2, (1, B // PAN // 2): 3, (2, 0): 4, (3, 0): 5}
+    steps = {(1, 0): 3, (2, 0): 4, (3, 0): 5}
 
     def hook(j, p):
         if (j, p) in steps:
@@ -245,8 +249,8 @@
     of_cross.land()
 
 
-def sums_and_factor(states_t, rates_t, count):
-    width = states_t.shape[1]
+def sums_and_factor(both_t, count):
+    width = both_t.shape[1]
     nb = width // B
     f32 = jnp.float32
     gram, cross = nb * (nb + 1) // 2 * B, nb * nb * B
@@ -262,7 +266,7 @@
     return pl.pallas_call(
         functools.partial(sums_kernel, nb, count),
         out_shape=[jax.ShapeDtypeStruct((gram, B), f32), jax.ShapeDtypeStruct((cross, B), f32)],
-        in_specs=[vmem] * 2,
+        in_specs=[vmem],
         out_specs=[vmem] * 2,
         scratch_shapes=[pltpu.VMEM((gram, B), f32)] * 2
         + landing(gram)
@@ -272,7 +276,7 @@
         compiler_params=pltpu.CompilerParams(
             collective_id=0, has_side_effects=True, vmem_limit_bytes=32 * 2**20
         ),
-    )(states_t, rates_t)
+    )(both_t)
 
 
 def substitute_kernel(nb, count, factor_ref, cross_ref, out_ref):
@@ -305,8 +309,8 @@
 
 def fast(snapshots, derivatives, basis):
     count = snapshots.shape[1] * lax.axis_size("tm")
-    states_t, rates_t = project_both(snapshots.T, derivatives.T, basis)
-    factor, cross = sums_and_factor(states_t, rates_t, count)
+    states_t, both_t = project_both(snapshots.T, derivatives.T, basis)
+    factor, cross = sums_and_factor(both_t, count)
     return states_t.T, substitute(factor, cross, basis.shape[1], count)
 
 

time: 79.4 us -> 73.1 us (0.921)
  Pallas kernels: 76.7 us -> 71.3 us
  local copies, waits for them, and re-layouts: 1.81 us -> 0.95 us
    pallas_call x1, Pallas kernels: 65.4 us -> 61.8 us  [sums_and_factor(): pl.pallas_call(functools.partial(sums_kernel, nb, count), out_shape=[jax....]
    pallas_call x1, Pallas kernels: 7.96 us -> 6.18 us  [project_both(): pl.pallas_call(project_kernel, grid=(depth // chunk,), out_shape=[jax.Sha...]
    unnamed x4 -> x2, local copies, waits for them, and re-layouts: 1.81 us -> 0.95 us
where the time goes in v3:
time: 73.1 us; the launch traced here: 72.9 us
  Pallas kernels  71.3 us (98%)
  local copies, waits for them, and re-layouts  0.95 us (1%)
    pallas_call x1, Pallas kernels, sums_and_factor(): pl.pallas_call(functools.partial(sums_kernel, nb, count), out_shape=[jax....  61.8 us
    pallas_call x1, Pallas kernels, project_both(): pl.pallas_call(project_kernel, grid=(depth // chunk,), out_shape=[jax.Sha...  6.18 us
    pallas_call x1, Pallas kernels, substitute(): pl.pallas_call(functools.partial(substitute_kernel, width // B, count), o...  3.34 us

profile of v3, /device:TPU:0, one launch (start us, length us, event | category | flops | bytes accessed | tf_op | source)
XLA Modules:
  0.0 72.9 jit_solution(2846751117531455303)
XLA Ops:
  0.6 6.2 %shard_map.50 = (f32[64,512]{1,0:T(8,128)}, f32[128,512]{1,0:T(8,128)}) custom-call(bf16[64,8192]{1,0:T(8,128)(2,1)} %bitcast.3, bf16[64,8192]{1,0:T(8,128)(2,1)} %bitcast.4, bf16[8192,512]{1,0:T(8,128)(2,1)} %basis.1), custom_call_target="tpu_custom_call" | custom-call | tf_op jit(solution)/shard_map/pallas_call | solution.py:56
  6.8 0.0 copy-start
  6.8 0.9 %copy-done = f32[128,512]{1,0:T(8,128)S(1)} copy-done((f32[128,512]{1,0:T(8,128)S(1)}, f32[128,512]{1,0:T(8,128)}, u32[]{:S(2)}) %copy-start) | copy-done | bytes 262168
  7.8 61.8 %shard_map.51 = (f32[1280,128]{1,0:T(8,128)S(1)}, f32[2048,128]{1,0:T(8,128)S(1)}) custom-call(f32[128,512]{1,0:T(8,128)S(1)} %copy-done), custom_call_target="tpu_custom_call" | custom-call | tf_op jit(solution)/shard_map/pallas_call | solution.py:266
  69.5 3.3 %shard_map.52 = f32[512,512]{1,0:T(8,128)} custom-call(f32[1280,128]{1,0:T(8,128)S(1)} %get-tuple-element.8.factor_ref, f32[2048,128]{1,0:T(8,128)S(1)} %get-tuple-element.9.cross_ref), custom_call_target="tpu_custom_call" | custom-call | tf_op jit(solution)/shard_map/pallas_call | solution.py:301
Async XLA Ops:
  6.8 0.9 %copy-start = (f32[128,512]{1,0:T(8,128)S(1)}, f32[128,512]{1,0:T(8,128)}, u32[]{:S(2)}) copy-start(f32[128,512]{1,0:T(8,128)} %get-tuple-element.7.both_ref) | copy-start | bytes 786436
